TPU v7x, 32 devices: a whole 2x2x4 slice. The times are simulated.
32 devices in a mesh: slab: 16 (over z, x, core), blk: 2 (over y).
Axes of the slice: x: 2, y: 2, z: 4, core: 2. Of those that a mesh axis runs over, the one named last changes fastest.
Arguments:
- modes: bfloat16 [65536, 2048], P('slab', 'blk'), may hold values from -6 to 6
- stiffness: bfloat16 [65536, 512], P('slab'), may hold values from -0.0009765625 to 0.0009765625
- offsets: int32 [1024, 8], P('slab'), may hold values from -4 to 4, as said below
Outputs:
- reduced: float32 [2048, 2048], P('blk', 'slab')
Inputs may be any that keep to these rules, and one draw needn't show every extreme that they name: Each row of offsets lists 8 different values, in an order drawn from the seed: all of -4 to 4 except one nonzero value of magnitude below 4.
All inputs are finite; a program needn't handle non-finite values.
Results may differ from a plain program's by a relative error of at most 0.0029.
Values may be sent and summed in bfloat16 or wider, within the bound.
No kernel may reach another device: no remote copies, remote signals or barrier semaphores. Data moves between devices by JAX's collectives and lax.ppermute only.
A program may use at most 192 MiB of HBM per device.

v0:
```python
import functools
import itertools

import jax
import jax.numpy as jnp
from jax import lax
from jax.experimental import pallas as pl
from jax.experimental.pallas import tpu as pltpu
from jax.sharding import PartitionSpec as P

BS = 64
HB = 4
BPR = 8
TILE = HB * BS
BAND = 3 * TILE
STEP = 4
AXES = ("slab", "blk")
F32 = jnp.float32
BF16 = jnp.bfloat16
NT = (((1,), (1,)), ((), ()))
TN = (((0,), (0,)), ((), ()))
VMEM_LIMIT = 56 * 1024 * 1024


def dot(a, b, dims=(((1,), (0,)), ((), ()))):
    return lax.dot_general(a, b, dims, preferred_element_type=F32)


def params():
    return pltpu.CompilerParams(vmem_limit_bytes=VMEM_LIMIT, dimension_semantics=("arbitrary",))


def plan_of(cols):
    if cols == 128:
        return (16, 32, 32, 48), ((0, 1), (2,), (3,))
    return (cols // 4,) * 4, ((0, 1), (2,), (3,))


def expand_kernel(count, off_ref, k_ref, out_ref, first_ref, held):
    step = pl.program_id(0)
    lower = lax.broadcasted_iota(jnp.int32, (BS, 2 * BS), 1) < BS
    held[...] = jnp.zeros_like(held)
    for row in range(count * HB):
        for pair in range(BPR // 2):
            straight = k_ref[row * BS : (row + 1) * BS, pair * 2 * BS : (pair + 1) * 2 * BS]
            swapped = pltpu.roll(straight.astype(F32), BS, 1).astype(BF16)
            for half in range(2):
                place = off_ref[step * (count * HB) + row, 2 * pair + half] + (HB + row % HB)
                held[row, place] = jnp.where((place & 1) == half, straight, swapped)
    for row in range(count * HB):
        rows = slice(row % HB * BS, (row % HB + 1) * BS)
        for pair in range(3 * HB // 2):
            out_ref[row // HB, rows, pair * 2 * BS : (pair + 1) * 2 * BS] = jnp.where(
                lower, held[row, 2 * pair], held[row, 2 * pair + 1]
            )

    @pl.when(step == 0)
    def _():
        first_ref[...] = out_ref[0, :, :TILE]


def expand(stiffness, offsets):
    rows = stiffness.shape[0]
    tiles = rows // TILE
    count = STEP
    return pl.pallas_call(
        functools.partial(expand_kernel, count),
        grid_spec=pltpu.PrefetchScalarGridSpec(
            num_scalar_prefetch=1,
            grid=(tiles // count,),
            in_specs=[pl.BlockSpec((count * TILE, BPR * BS), lambda t, off: (t, 0))],
            out_specs=[
                pl.BlockSpec((count, TILE, BAND), lambda t, off: (t, 0, 0)),
                pl.BlockSpec((TILE, TILE), lambda t, off: (0, 0)),
            ],
            scratch_shapes=[pltpu.VMEM((count * HB, 3 * HB, BS, 2 * BS), BF16)],
        ),
        out_shape=[jax.ShapeDtypeStruct((tiles, TILE, BAND), BF16), jax.ShapeDtypeStruct((TILE, TILE), BF16)],
        compiler_params=params(),
        name="expand_band",
    )(offsets, stiffness)


def copy_kernel(at_ref, from_ref, to_ref):
    to_ref[...] = from_ref[...]


def take_tile(modes, at):
    block = (TILE, modes.shape[1])
    return pl.pallas_call(
        copy_kernel,
        grid_spec=pltpu.PrefetchScalarGridSpec(
            num_scalar_prefetch=1,
            grid=(1,),
            in_specs=[pl.BlockSpec(block, lambda t, at: (at[0], 0))],
            out_specs=pl.BlockSpec(block, lambda t, at: (0, 0)),
        ),
        out_shape=jax.ShapeDtypeStruct(block, modes.dtype),
        compiler_params=params(),
        name="take_tile",
    )(at, modes)


def fold_kernel(at_ref, keep_ref, came_keep_ref, give_ref, came_give_ref, kept_ref, given_ref):
    kept_ref[...] = keep_ref[...] + came_keep_ref[...].astype(F32)
    given_ref[...] = (give_ref[...] + came_give_ref[...].astype(F32)).astype(given_ref.dtype)


def fold(at, held, came, wire):
    count, _, rows, cols = held.shape
    block = (count, pl.squeezed, rows, cols)
    keep = pl.BlockSpec(block, lambda t, at: (0, at[0], 0, 0))
    give = pl.BlockSpec(block, lambda t, at: (0, 1 - at[0], 0, 0))
    out = pl.BlockSpec((count, rows, cols), lambda t, at: (0, 0, 0))
    return pl.pallas_call(
        fold_kernel,
        grid_spec=pltpu.PrefetchScalarGridSpec(
            num_scalar_prefetch=1, grid=(1,), in_specs=[keep, keep, give, give], out_specs=[out, out]
        ),
        out_shape=[jax.ShapeDtypeStruct((count, rows, cols), kind) for kind in (F32, wire)],
        compiler_params=params(),
        name="fold",
    )(at, held, came, held, came)


def deal_out_kernel(at_ref, mine_ref, came_ref, out_ref):
    panel = pl.program_id(0)
    total = mine_ref[0] + came_ref[0].astype(F32)
    ours = jnp.logical_or(panel == at_ref[0], panel == at_ref[1])
    out_ref[0] = jnp.where(ours, total, 0).astype(BF16)


def deal_out_sums(at, mine, came, panels):
    block = (1, *mine.shape[1:])
    part = pl.BlockSpec(block, lambda panel, at: (jnp.where(panel == at[0], 0, 1), 0, 0, 0))
    return pl.pallas_call(
        deal_out_kernel,
        grid_spec=pltpu.PrefetchScalarGridSpec(
            num_scalar_prefetch=1,
            grid=(panels,),
            in_specs=[part, part],
            out_specs=pl.BlockSpec(block, lambda panel, at: (panel, 0, 0, 0)),
        ),
        out_shape=jax.ShapeDtypeStruct((panels, *mine.shape[1:]), BF16),
        compiler_params=params(),
        name="deal_out_sums",
    )(at, mine, came)


def gather_up_kernel(came_ref, out_ref):
    out_ref[...] = jnp.sum(came_ref[...].astype(F32), axis=0)


def gather_up_sums(came):
    return pl.pallas_call(
        gather_up_kernel,
        out_shape=jax.ShapeDtypeStruct(came.shape[1:], F32),
        compiler_params=pltpu.CompilerParams(vmem_limit_bytes=VMEM_LIMIT),
        name="gather_up_sums",
    )(came)


def turn_kernel(cols, widths, at_ref, m_ref, *out_refs):
    for slab in range(m_ref.shape[1] // cols):
        turned = m_ref[:, slab * cols : (slab + 1) * cols].T
        start = 0
        for width, out_ref in zip(widths, out_refs):
            out_ref[slab * width : (slab + 1) * width, :] = turned[start : start + width, :]
            start += width


def turn(modes, rows, at, cols, widths):
    panel = modes.shape[1]
    slabs = panel // cols
    block = min(rows, STEP * TILE)
    steps = rows // block
    return pl.pallas_call(
        functools.partial(turn_kernel, cols, widths),
        grid_spec=pltpu.PrefetchScalarGridSpec(
            num_scalar_prefetch=1,
            grid=(steps,),
            in_specs=[pl.BlockSpec((block, panel), lambda t, at: (at[0] * steps + t, 0))],
            out_specs=[pl.BlockSpec((slabs * w, block), lambda t, at: (0, t)) for w in widths],
        ),
        out_shape=[jax.ShapeDtypeStruct((slabs * w, rows), BF16) for w in widths],
        compiler_params=params(),
        name="turn",
    )(at, modes)


def deal(core, both, mine_ref, theirs_ref, index):
    even, odd = both
    mine_ref[index] = jnp.where(core == 0, even, odd)
    theirs_ref[index] = jnp.where(core == 0, odd, even).astype(theirs_ref.dtype)


def kphi_kernel(steps, kb_ref, prev_ref, cur_ref, next_ref, left_ref, right_ref, z_ref):
    t = pl.program_id(0)
    before = jnp.where(t == 0, left_ref[...], prev_ref[...])
    after = jnp.where(t == steps - 1, right_ref[...], next_ref[...])
    window = jnp.concatenate([before, cur_ref[...], after], axis=0)
    for tile in range(STEP):
        rows = slice(tile * TILE, (tile + 1) * TILE)
        z_ref[rows, :] = dot(kb_ref[tile], window[tile * TILE : tile * TILE + BAND]).astype(BF16)


def own_kphi(band, modes, left, right):
    rows, panel = modes.shape
    tiles = rows // TILE
    steps = tiles // STEP
    whole = pl.BlockSpec((TILE, panel), lambda t: (0, 0))
    return pl.pallas_call(
        functools.partial(kphi_kernel, steps),
        grid=(steps,),
        in_specs=[
            pl.BlockSpec((STEP, TILE, BAND), lambda t: (t, 0, 0)),
            pl.BlockSpec((TILE, panel), lambda t: (jnp.maximum(t * STEP - 1, 0), 0)),
            pl.BlockSpec((STEP * TILE, panel), lambda t: (t, 0)),
            pl.BlockSpec((TILE, panel), lambda t: (jnp.minimum((t + 1) * STEP, tiles - 1), 0)),
            whole,
            whole,
        ],
        out_specs=pl.BlockSpec((STEP * TILE, panel), lambda t: (t, 0)),
        out_shape=jax.ShapeDtypeStruct((rows, panel), BF16),
        compiler_params=params(),
        name="own_kphi",
    )(band, modes, modes, modes, left, right)


def square_kernel(steps, cols, at_ref, m_ref, z_ref, mine_ref, theirs_ref, acc):
    t = pl.program_id(0)

    @pl.when(t == 0)
    def _():
        acc[...] = jnp.zeros_like(acc)

    acc[...] += dot(m_ref[...], z_ref[...], TN)

    @pl.when(t == steps - 1)
    def _():
        for pair in range(mine_ref.shape[0]):
            first = 2 * pair * cols
            deal(at_ref[0], (acc[:, first : first + cols], acc[:, first + cols : first + 2 * cols]), mine_ref, theirs_ref, pair)


def own_square(core, modes, kphi, cols):
    rows, panel = modes.shape
    steps = rows // TILE // STEP
    pairs = panel // cols // 2
    here = pl.BlockSpec((STEP * TILE, panel), lambda t, at: (t, 0))
    dealt = pl.BlockSpec((pairs, panel, cols), lambda t, at: (0, 0, 0))
    return pl.pallas_call(
        functools.partial(square_kernel, steps, cols),
        grid_spec=pltpu.PrefetchScalarGridSpec(
            num_scalar_prefetch=1,
            grid=(steps,),
            in_specs=[here, here],
            out_specs=[dealt, dealt],
            scratch_shapes=[pltpu.VMEM((panel, panel), F32)],
        ),
        out_shape=[jax.ShapeDtypeStruct((pairs, panel, cols), kind) for kind in (F32, BF16)],
        compiler_params=params(),
        name="own_square",
    )(core, modes, kphi)


def pair_kernel(steps, cols, widths, at_ref, kb_ref, *refs):
    pieces = len(widths)
    prevs, curs, nexts, rights = (refs[i * pieces : (i + 1) * pieces] for i in range(4))
    m_ref, z_ref, mid_ref, reach_ref, last_ref, mine_ref, theirs_ref, own, cross = refs[4 * pieces :]
    t = pl.program_id(0)
    join = lambda parts: jnp.concatenate([part[...] for part in parts], axis=0)
    cur, right = join(curs), join(rights)
    before = join(prevs)
    before = jnp.where(t == 0, jnp.zeros_like(before), before)
    after = jnp.where(t == steps - 1, right, join(nexts))
    window = jnp.concatenate([before, cur, after], axis=1)
    kx = [dot(window[:, tile * TILE : tile * TILE + BAND], kb_ref[tile], NT).astype(BF16) for tile in range(STEP)]

    @pl.when(t == 0)
    def _():
        own[...] = jnp.zeros_like(own)
        edge = jnp.where(at_ref[1] == 0, mid_ref[0], reach_ref[...])
        cross[...] = dot(right, dot(edge, last_ref[...]).astype(BF16))

    own[...] += dot(jnp.concatenate(kx, axis=1), m_ref[...])
    cross[...] += dot(cur, z_ref[...])

    @pl.when(t == steps - 1)
    def _():
        pairs = mine_ref.shape[1]
        for piece, slab in itertools.product(range(pieces), range(2 * pairs)):
            width = widths[piece]
            lead = 2 * pairs * sum(widths[:piece])
            rows = lambda where: slice(lead + where * width, lead + (where + 1) * width)
            lanes = lambda where: slice(where * cols, (where + 1) * cols)
            start = slab * sum(widths) + sum(widths[:piece])
            to = slice(start, start + width)
            for pair in range(pairs):
                ends = (2 * pair, 2 * pair + 1)
                deal(at_ref[0], [cross[rows(slab), lanes(end)] for end in ends], mine_ref, theirs_ref, (0, pair, to))
                deal(at_ref[0], [own[rows(end), lanes(slab)] for end in ends], mine_ref, theirs_ref, (1, pair, to))


def pair_products(at, band, turned, turned_right, modes, kphi, reach, cols, widths):
    rows, panel = modes.shape
    tiles = rows // TILE // 2
    steps = tiles // STEP
    slabs = panel // cols
    some = [slabs * width for width in widths]
    count = sum(some)
    dealt = pl.BlockSpec((2, slabs // 2, count, cols), lambda t, at: (0, 0, 0, 0))
    here = pl.BlockSpec((STEP * TILE, panel), lambda t, at: (at[1] * steps + t, 0))
    return pl.pallas_call(
        functools.partial(pair_kernel, steps, cols, widths),
        grid_spec=pltpu.PrefetchScalarGridSpec(
            num_scalar_prefetch=1,
            grid=(steps,),
            in_specs=[
                pl.BlockSpec((STEP, TILE, BAND), lambda t, at: (at[1] * steps + t, 0, 0)),
                *[pl.BlockSpec((n, TILE), lambda t, at: (0, jnp.maximum(t * STEP - 1, 0))) for n in some],
                *[pl.BlockSpec((n, STEP * TILE), lambda t, at: (0, t)) for n in some],
                *[pl.BlockSpec((n, TILE), lambda t, at: (0, jnp.minimum((t + 1) * STEP, tiles - 1))) for n in some],
                *[pl.BlockSpec((n, TILE), lambda t, at: (0, 0)) for n in some],
                here,
                here,
                pl.BlockSpec((1, TILE, TILE), lambda t, at: (tiles, 0, 0)),
                pl.BlockSpec((TILE, TILE), lambda t, at: (0, 0)),
                pl.BlockSpec((TILE, panel), lambda t, at: (at[1] * tiles + tiles - 1, 0)),
            ],
            out_specs=[dealt, dealt],
            scratch_shapes=[pltpu.VMEM((count, panel), F32)] * 2,
        ),
        out_shape=[jax.ShapeDtypeStruct((2, slabs // 2, count, cols), kind) for kind in (F32, BF16)],
        compiler_params=params(),
        name="pair_products",
    )(at, band, *turned, *turned, *turned, *turned_right, modes, kphi, band, reach, modes)


class Places:
    def __init__(self, mesh):
        self.slabs = mesh.shape["slab"]
        self.panels = mesh.shape["blk"]
        self.group = self.slabs // self.panels
        self.all = [(s, b) for s in range(self.slabs) for b in range(self.panels)]

    def send(self, value, pairs):
        flat = [(s * self.panels + b, t * self.panels + c) for (s, b), (t, c) in pairs]
        return lax.ppermute(value, AXES, flat)

    def across(self, value, bit):
        return self.send(value, [((s, b), (s ^ bit, b)) for s, b in self.all])


def pick(array, index, axis=0):
    return lax.dynamic_index_in_dim(array, index, axis, keepdims=False)


def tie(value, *others):
    return lax.optimization_barrier((value, others))[0]


def body(places, modes, stiffness, offsets):
    rows, panel = modes.shape
    group, panels, slabs = places.group, places.panels, places.slabs
    cols = panel // group
    widths, groups = plan_of(cols)
    half = rows // 2
    slab, b = lax.axis_index("slab"), lax.axis_index("blk")
    p, core = slab // group, slab % 2
    one = lambda *values: jnp.stack([jnp.asarray(v, jnp.int32) for v in values])
    core_at, x_at, z_at, panel_at = one(core), one(slab // 2 % 2), one(slab // 4 % 2), one(jnp.where(p == b, 0, 1))
    zl = group // 4

    rights, ready = [], []
    for k in range(1, panels):
        pairs = []
        for s, c in places.all:
            other = (c - k) % panels
            if c < other:
                pairs.append(((s, other), (s, c)))
            elif s + 1 < slabs:
                pairs.append(((s + 1, other), (s, c)))
        tile = take_tile(modes, one(jnp.where((b + k) % panels < b, half // TILE, 0)))
        rights.append(places.send(tile, pairs))
    for k in range(1, panels):
        ready.append(turn(modes, half, one(jnp.where((b + k) % panels < b, 0, 1)), cols, widths))
    to_right = [((s, c), (s + 1, c)) for s, c in places.all if s + 1 < slabs]
    to_left = [(there, here) for here, there in to_right]
    left = places.send(tie(modes[rows - TILE :], ready), to_right)
    right = places.send(tie(modes[:TILE], ready), to_left)
    stiffness, ready = lax.optimization_barrier((stiffness, ready))
    band, first_band = expand(stiffness, offsets)
    reach = places.send(first_band, to_left)

    own = jnp.zeros((group, cols, cols), F32)
    cross = jnp.zeros((group, cols, cols), F32)
    for k in range(1, panels):
        other = (b - k) % panels
        source = (b + k) % panels
        at = one(core, jnp.where(b < other, 0, 1))
        there = [((s, c), (s, (c + k) % panels)) for s, c in places.all]
        same_core = [list(range(first, slabs, 2)) for first in range(2)]
        pieces = ready[k - 1]

        arrived = [places.send(pieces[0], there)]
        arrived.append(places.send(tie(pieces[1], arrived[0], left, right, rights, band), there))
        if k == 1:
            kphi = own_kphi(tie(band, rights, arrived[0]), modes, left, right)
        turned_rights = turn(rights[k - 1], TILE, one(0), cols, widths)
        arrived.append(places.send(tie(pieces[2], kphi), there))
        if k == 1:
            square = own_square(core_at, modes, tie(kphi, reach), cols)
        for piece in pieces[3:]:
            arrived.append(places.send(tie(piece, arrived[len(arrived) - 2]), there))

        def multiply(members, *gates):
            took = [tie(arrived[piece], *gates) for piece in members]
            tails = [turned_rights[piece] for piece in members]
            return pair_products(at, band, took, tails, modes, kphi, reach, cols, [widths[piece] for piece in members])

        def over_core(mine, theirs):
            return deal_out_sums(one(b, other), mine, places.across(theirs, 1), panels)

        def deal_out(parts):
            parts = parts.reshape(slabs // 2, *parts.shape[2:])
            return lax.all_to_all(parts, "slab", 0, 0, axis_index_groups=same_core)

        def gather_up(came, *gates):
            return gather_up_sums(tie(came, *gates)).reshape(group, -1, cols)

        def square_over(kept, given, bit, where, wire=BF16):
            shape = (-1, 2, *kept.shape[-2:])
            return fold(where, kept.reshape(shape), places.across(given, bit).reshape(shape), wire)

        def square_over_panels(kept, given):
            total = kept[0] + places.across(given, 4)[0].astype(F32) if group > 4 else kept[0]
            wire = total.astype(BF16)
            for d in range(1, panels):
                goal = lambda s: (s + d * group) % slabs
                pairs = [((s, c), (goal(s), c)) for s, c in places.all if goal(s) // group == c]
                total = total + places.send(wire, pairs).astype(F32)
            return total

        mine, theirs = multiply(groups[0], square[1])
        if k == 1:
            square_sum = square_over(*square, 1, x_at)
        first = over_core(mine, tie(theirs, arrived[groups[1][0]]))
        mine, theirs = multiply(groups[1], first, square_sum if k == 1 else ())
        first = gather_up(deal_out(first))
        second = over_core(mine, theirs)
        if k == 1:
            kept, given = square_sum
            square_sum = square_over(kept, given, 2, z_at) if group > 4 else [kept + places.across(given, 2).astype(F32)] * 2
        mine, theirs = multiply(groups[2], second)
        second = deal_out(second)
        third = deal_out(over_core(mine, tie(theirs, first, square_sum if k == 1 else ())))
        if k == 1:
            square_sum = square_over_panels(*square_sum)
        second = gather_up(second)
        third = gather_up(third, second)
        if k == 1:
            total_square = square_sum
        pairs = [((s, c), (s, (c - k) % panels)) for s, c in places.all if s // group == c]
        early = jnp.concatenate((first, second), 1)
        early_came = places.send(early, pairs)
        late = tie(third, early_came)
        came = jnp.concatenate([early_came, places.send(late, pairs)], 1)
        own = own + jnp.where(p == other, jnp.concatenate([early, late], 1), 0)
        cross = cross + jnp.where(p == source, came, 0)

    off = (jnp.swapaxes(own, 1, 2) + cross).reshape(panel, cols)
    return jnp.where(p == b, total_square, off)


def solution(mesh):
    in_specs = (P("slab", "blk"), P("slab", None), P("slab", None))
    out_specs = P("blk", "slab")
    return jax.shard_map(
        functools.partial(body, Places(mesh)), mesh=mesh, in_specs=in_specs, out_specs=out_specs, check_vma=False
    )
```

profile of v0, /device:TPU:0, one launch (start us, length us, event | category | flops | bytes accessed | tf_op | source)
XLA Modules:
  0.0 198.1 jit_solution(860242889871956933)
XLA Ops:
  0.0 1.9 take_tile.1
  1.9 1.3 collective-permute-start
  3.2 4.2 %turn.2 = (bf16[128,2048]{1,0:T(8,128)(2,1)}, bf16[256,2048]{1,0:T(8,128)(2,1)}, bf16[256,2048]{1,0:T(8,128)(2,1)}, bf16[384,2048]{1,0:T(8,128)(2,1)}) custom-call(s32[1]{0:T(128)} %bitcast.3.at_ref, bf16[4096,1024]{1,0:T(8,128)(2,1)} %refs_8_.5), custom_call_target="tpu_custom_call" | custom-call | tf_op jit(solution)/shard_map/turn/pallas_call | solution.py:177
  7.4 3.6 %collective-permute-start.1 = (bf16[128,2048]{1,0:T(8,128)(2,1)}, bf16[128,2048]{1,0:T(8,128)(2,1)S(1)}, u32[]{:S(2)}, u32[]{:S(2)}) collective-permute-start(bf16[128,2048]{1,0:T(8,128)(2,1)} %get-tuple-element.53), channel_id=1, source_target_pairs={{0,1},{1,0},{2,3},{3,2},{4,5},{5,4},{6,7},{7,6},{8,9},{9,8},{10,11... | collective-permute-start | bytes 1572872 | tf_op jit(solution)/shard_map/ppermute | solution.py:349
  11.0 1.3 fusion.2
  12.2 2.0 %collective-permute-start.2 = (bf16[256,1024]{1,0:T(8,128)(2,1)S(1)}, bf16[256,1024]{1,0:T(8,128)(2,1)S(1)}, u32[]{:S(2)}, u32[]{:S(2)}) collective-permute-start(bf16[256,1024]{1,0:T(8,128)(2,1)S(1)} %get-tuple-element.55), channel_id=1, source_target_pairs={{0,2},{1,3},{2,4},{3,5},{4,6},{5,7},{6,8},{7,9},{8,10},{9,11},{10,... | collective-permute-start | bytes 1572872 | tf_op jit(solution)/shard_map/ppermute | solution.py:349
  14.3 1.3 collective-permute-start.3
  16.3 9.4 %expand_band.1 = (bf16[16,256,768]{2,1,0:T(8,128)(2,1)}, bf16[256,256]{1,0:T(8,128)(2,1)}) custom-call(s32[64,8]{1,0:T(8,128)} %copy.4.off_ref, bf16[4096,512]{1,0:T(8,128)(2,1)} %k_ref), custom_call_target="tpu_custom_call" | custom-call | tf_op jit(solution)/shard_map/expand_band/pallas_call | solution.py:66
  25.6 4.4 %collective-permute-done.1.refs_0_.refs_2_.refs_4_ = bf16[128,2048]{1,0:T(8,128)(2,1)S(1)} collective-permute-done((bf16[128,2048]{1,0:T(8,128)(2,1)}, bf16[128,2048]{1,0:T(8,128)(2,1)S(1)}, u32[]{:S(2)}, u32[]{:S(2)}) %collective-permute-start.1) | collective-permute-done | bytes 524320 | tf_op jit(solution)/shard_map/ppermute | solution.py:349
  31.1 13.9 %own_kphi.1.z_ref.refs_9_.refs_5_ = bf16[4096,1024]{1,0:T(8,128)(2,1)} custom-call(bf16[16,256,768]{2,1,0:T(8,128)(2,1)} %get-tuple-element.54.kb_ref.refs_10_.refs_6_, bf16[4096,1024]{1,0:T(8,128)(2,1)} %refs_8_.5, bf16[4096,1024]{1,0:T(8,128)(2,1)} %refs_8_.5, bf16[4096,1024]{1,0:T(8,128)(2,1)} %refs_8_.5, bf16[256,1024]{1,0:T(8,128)(2,1)} %copy-done.14, ...), custom_call_target="tpu_custom_call" | custom-call | tf_op jit(solution)/shard_map/own_kphi/pallas_call | solution.py:212
  45.0 1.1 collective-permute-start.10
  46.2 1.3 collective-permute-start.4
  48.1 1.6 collective-permute-done.4.refs_11_.refs_7_
  49.7 14.1 %own_square.1 = (f32[4,1024,128]{2,1,0:T(8,128)}, bf16[4,1024,128]{2,1,0:T(8,128)(2,1)}) custom-call(s32[1]{0:T(128)} %bitcast.2.at_ref, bf16[4096,1024]{1,0:T(8,128)(2,1)} %refs_8_.5, bf16[4096,1024]{1,0:T(8,128)(2,1)} %own_kphi.1.z_ref.refs_9_.refs_5_), custom_call_target="tpu_custom_call" | custom-call | tf_op jit(solution)/shard_map/own_square/pallas_call | solution.py:252
  63.7 2.0 %turn.3 = (bf16[128,256]{1,0:T(8,128)(2,1)}, bf16[256,256]{1,0:T(8,128)(2,1)}, bf16[256,256]{1,0:T(8,128)(2,1)}, bf16[384,256]{1,0:T(8,128)(2,1)}) custom-call(s32[1]{0:T(128)} %constant.78.clone.1.at_ref, bf16[256,1024]{1,0:T(8,128)(2,1)} %copy-done.17), custom_call_target="tpu_custom_call" | custom-call | tf_op jit(solution)/shard_map/turn/pallas_call | solution.py:177
  65.8 1.0 copy-done.2
  66.7 12.2 %pair_products.3 = (f32[2,4,384,128]{3,2,1,0:T(8,128)}, bf16[2,4,384,128]{3,2,1,0:T(8,128)(2,1)}) custom-call(s32[2]{0:T(128)} %pad_add_fusion.1.at_ref, bf16[16,256,768]{2,1,0:T(8,128)(2,1)} %get-tuple-element.54.kb_ref.refs_10_.refs_6_, bf16[128,2048]{1,0:T(8,128)(2,1)} %copy-done.3, bf16[256,2048]{1,0:T(8,128)(2,1)} %copy-done.2, ...), custom_call_target="tpu_custom_call" | custom-call | tf_op jit(solution)/shard_map/pair_products/pallas_call | solution.py:314
  79.0 3.9 %collective-permute-start.11 = (bf16[2,4,384,128]{3,2,1,0:T(8,128)(2,1)}, bf16[2,4,384,128]{3,2,1,0:T(8,128)(2,1)S(1)}, u32[]{:S(2)}, u32[]{:S(2)}) collective-permute-start(bf16[2,4,384,128]{3,2,1,0:T(8,128)(2,1)} %get-tuple-element.75), channel_id=1, source_target_pairs={{0,2},{1,3},{2,0},{3,1},{4,6},{5,7},{6,4},{7,5},{8,10},{9,11},{10,... | collective-permute-start | bytes 2359304 | tf_op jit(solution)/shard_map/ppermute | solution.py:349
  84.4 1.0 collective-permute-done.11.came_ref
  85.4 1.0 copy-done.12
  86.3 3.1 %deal_out_sums.3 = bf16[2,4,384,128]{3,2,1,0:T(8,128)(2,1)} custom-call(s32[2]{0:T(128)} %pad_add_fusion.at_ref, f32[2,4,384,128]{3,2,1,0:T(8,128)} %get-tuple-element.71.mine_ref, bf16[2,4,384,128]{3,2,1,0:T(8,128)(2,1)} %copy-done.12), custom_call_target="tpu_custom_call" | custom-call | tf_op jit(solution)/shard_map/deal_out_sums/pallas_call | solution.py:136
  89.4 5.4 %all-to-all-start = ((bf16[8,384,128]{2,1,0:T(8,128)(2,1)}), bf16[8,384,128]{2,1,0:T(8,128)(2,1)S(1)}, u32[]{:S(2)}, u32[]{:S(2)}) async-start(bf16[8,384,128]{2,1,0:T(8,128)(2,1)} %bitcast.33), calls=%async_computation | async-start | bytes 1572864 | tf_op jit(solution)/shard_map/all_to_all | solution.py:427
  94.8 3.1 %fold.2 = (f32[2,1024,128]{2,1,0:T(8,128)}, bf16[2,1024,128]{2,1,0:T(8,128)(2,1)}) custom-call(s32[1]{0:T(128)} %bitcast.1.at_ref, f32[2,2,1024,128]{3,2,1,0:T(8,128)} %bitcast.29, bf16[2,2,1024,128]{3,2,1,0:T(8,128)(2,1)} %bitcast.6.came_keep_ref.came_give_ref, f32[2,2,1024,128]{3,2,1,0:T(8,128)} %bitcast.30, ...), custom_call_target="tpu_custom_call" | custom-call | tf_op jit(solution)/shard_map/fold/pallas_call | solution.py:115
  97.9 9.6 %pair_products.4 = (f32[2,4,256,128]{3,2,1,0:T(8,128)}, bf16[2,4,256,128]{3,2,1,0:T(8,128)(2,1)}) custom-call(s32[2]{0:T(128)} %pad_add_fusion.1.at_ref, bf16[16,256,768]{2,1,0:T(8,128)(2,1)} %get-tuple-element.54.kb_ref.refs_10_.refs_6_, bf16[256,2048]{1,0:T(8,128)(2,1)} %copy-done.1, bf16[256,2048]{1,0:T(8,128)(2,1)} %copy-done.1, ...), custom_call_target="tpu_custom_call" | custom-call | tf_op jit(solution)/shard_map/pair_products/pallas_call | solution.py:314
  107.6 2.0 %collective-permute-start.6 = (bf16[2,1024,128]{2,1,0:T(8,128)(2,1)}, bf16[2,1024,128]{2,1,0:T(8,128)(2,1)S(1)}, u32[]{:S(2)}, u32[]{:S(2)}) collective-permute-start(bf16[2,1024,128]{2,1,0:T(8,128)(2,1)} %get-tuple-element.62), channel_id=1, source_target_pairs={{0,4},{1,5},{2,6},{3,7},{4,0},{5,1},{6,2},{7,3},{8,12},{9,13},{10,... | collective-permute-start | bytes 1572872 | tf_op jit(solution)/shard_map/ppermute | solution.py:349
  110.5 2.8 %deal_out_sums.4 = bf16[2,4,256,128]{3,2,1,0:T(8,128)(2,1)} custom-call(s32[2]{0:T(128)} %pad_add_fusion.at_ref, f32[2,4,256,128]{3,2,1,0:T(8,128)} %get-tuple-element.78.mine_ref, bf16[2,4,256,128]{3,2,1,0:T(8,128)(2,1)} %copy-done.16), custom_call_target="tpu_custom_call" | custom-call | tf_op jit(solution)/shard_map/deal_out_sums/pallas_call | solution.py:136
  113.3 2.2 %all-to-all-done.came_ref = bf16[8,384,128]{2,1,0:T(8,128)(2,1)S(1)} async-done(((bf16[8,384,128]{2,1,0:T(8,128)(2,1)}), bf16[8,384,128]{2,1,0:T(8,128)(2,1)S(1)}, u32[]{:S(2)}, u32[]{:S(2)}) %all-to-all-start) | async-done | bytes 786464 | tf_op jit(solution)/shard_map/all_to_all | solution.py:427
  115.5 3.8 %all-to-all-start.1 = ((bf16[8,256,128]{2,1,0:T(8,128)(2,1)}), bf16[8,256,128]{2,1,0:T(8,128)(2,1)S(1)}, u32[]{:S(2)}, u32[]{:S(2)}) async-start(bf16[8,256,128]{2,1,0:T(8,128)(2,1)} %bitcast.35), calls=%async_computation.1 | async-start | bytes 1048576 | tf_op jit(solution)/shard_map/all_to_all | solution.py:427
  119.3 7.2 %collective-permute-done.6 = bf16[2,1024,128]{2,1,0:T(8,128)(2,1)S(1)} collective-permute-done((bf16[2,1024,128]{2,1,0:T(8,128)(2,1)}, bf16[2,1024,128]{2,1,0:T(8,128)(2,1)S(1)}, u32[]{:S(2)}, u32[]{:S(2)}) %collective-permute-start.6) | collective-permute-done | bytes 524320 | tf_op jit(solution)/shard_map/ppermute | solution.py:349
  127.3 2.3 %fold.3 = (f32[1,1024,128]{2,1,0:T(8,128)}, bf16[1,1024,128]{2,1,0:T(8,128)(2,1)}) custom-call(s32[1]{0:T(128)} %bitcast.at_ref, f32[1,2,1024,128]{3,2,1,0:T(8,128)} %bitcast.31, bf16[1,2,1024,128]{3,2,1,0:T(8,128)(2,1)} %bitcast.36, f32[1,2,1024,128]{3,2,1,0:T(8,128)} %bitcast.32, bf16[1,2,1024,128]{3,2,1,0:T(8,128)(2,1)} %bitcast.37), custom_call_target="tpu_custom_call" | custom-call | tf_op jit(solution)/shard_map/fold/pallas_call | solution.py:115
  129.6 1.2 copy-done
  130.7 11.8 %pair_products.5 = (f32[2,4,384,128]{3,2,1,0:T(8,128)}, bf16[2,4,384,128]{3,2,1,0:T(8,128)(2,1)}) custom-call(s32[2]{0:T(128)} %pad_add_fusion.1.at_ref, bf16[16,256,768]{2,1,0:T(8,128)(2,1)} %get-tuple-element.54.kb_ref.refs_10_.refs_6_, bf16[384,2048]{1,0:T(8,128)(2,1)} %copy-done, bf16[384,2048]{1,0:T(8,128)(2,1)} %copy-done, bf16[384,2048]{1,0:T(8,128)(2,1)} %copy-done, ...), custom_call_target="tpu_custom_call" | custom-call | tf_op jit(solution)/shard_map/pair_products/pallas_call | solution.py:314
  142.5 1.9 gather_up_sums.3
  144.4 2.5 %collective-permute-done.14.came_ref = bf16[2,4,384,128]{3,2,1,0:T(8,128)(2,1)S(1)} collective-permute-done((bf16[2,4,384,128]{3,2,1,0:T(8,128)(2,1)}, bf16[2,4,384,128]{3,2,1,0:T(8,128)(2,1)S(1)}, u32[]{:S(2)}, u32[]{:S(2)}) %collective-permute-start.14) | collective-permute-done | bytes 786464 | tf_op jit(solution)/shard_map/ppermute | solution.py:349
  146.9 0.9 copy-done.13
  147.8 3.3 %deal_out_sums.5 = bf16[2,4,384,128]{3,2,1,0:T(8,128)(2,1)} custom-call(s32[2]{0:T(128)} %pad_add_fusion.at_ref, f32[2,4,384,128]{3,2,1,0:T(8,128)} %get-tuple-element.84.mine_ref, bf16[2,4,384,128]{3,2,1,0:T(8,128)(2,1)} %copy-done.13), custom_call_target="tpu_custom_call" | custom-call | tf_op jit(solution)/shard_map/deal_out_sums/pallas_call | solution.py:136
  151.9 5.0 %all-to-all-start.2 = ((bf16[8,384,128]{2,1,0:T(8,128)(2,1)}), bf16[8,384,128]{2,1,0:T(8,128)(2,1)S(1)}, u32[]{:S(2)}, u32[]{:S(2)}) async-start(bf16[8,384,128]{2,1,0:T(8,128)(2,1)} %bitcast.34), calls=%async_computation.2 | async-start | bytes 1572864 | tf_op jit(solution)/shard_map/all_to_all | solution.py:427
  157.1 1.8 gather_up_sums.4
  158.8 1.2 copy.6
  160.2 2.8 %collective-permute-start.15 = (f32[8,80,128]{1,2,0:T(8,128)S(1)}, f32[8,80,128]{1,2,0:T(8,128)S(1)}, u32[]{:S(2)}, u32[]{:S(2)}) collective-permute-start(f32[8,80,128]{1,2,0:T(8,128)S(1)} %pad_maximum_fusion), channel_id=1, source_target_pairs={{0,1},{2,3},{4,5},{6,7},{8,9},{10,11},{12,13},{14,15},{17,16},{19,... | collective-permute-start | bytes 983048 | tf_op jit(solution)/shard_map/ppermute | solution.py:349
  163.0 2.1 %collective-permute-start.7 = (bf16[1,1024,128]{2,1,0:T(8,128)(2,1)S(1)}, bf16[1,1024,128]{2,1,0:T(8,128)(2,1)S(1)}, u32[]{:S(2)}, u32[]{:S(2)}) collective-permute-start(bf16[1,1024,128]{2,1,0:T(8,128)(2,1)S(1)} %copy-done.19), channel_id=1, source_target_pairs={{0,8},{1,9},{2,10},{3,11},{4,12},{5,13},{6,14},{7,15},{8,0},{9,1},... | collective-permute-start | bytes 786440 | tf_op jit(solution)/shard_map/ppermute | solution.py:349
  165.1 12.3 %all-to-all-done.2.came_ref = bf16[8,384,128]{2,1,0:T(8,128)(2,1)S(1)} async-done(((bf16[8,384,128]{2,1,0:T(8,128)(2,1)}), bf16[8,384,128]{2,1,0:T(8,128)(2,1)S(1)}, u32[]{:S(2)}, u32[]{:S(2)}) %all-to-all-start.2) | async-done | bytes 786464 | tf_op jit(solution)/shard_map/all_to_all | solution.py:427
  178.3 1.9 gather_up_sums.5
  180.2 2.7 %collective-permute-start.16 = (f32[8,48,128]{2,1,0:T(8,128)}, f32[8,48,128]{2,1,0:T(8,128)S(1)}, u32[]{:S(2)}, u32[]{:S(2)}) collective-permute-start(f32[8,48,128]{2,1,0:T(8,128)} %bitcast.42), channel_id=1, source_target_pairs={{0,1},{2,3},{4,5},{6,7},{8,9},{10,11},{12,13},{14,15},{17,16},{19,... | collective-permute-start | bytes 589832 | tf_op jit(solution)/shard_map/ppermute | solution.py:349
  183.1 1.3 collective-permute-start.8
  184.4 2.1 %collective-permute-done.16 = f32[8,48,128]{2,1,0:T(8,128)S(1)} collective-permute-done((f32[8,48,128]{2,1,0:T(8,128)}, f32[8,48,128]{2,1,0:T(8,128)S(1)}, u32[]{:S(2)}, u32[]{:S(2)}) %collective-permute-start.16) | collective-permute-done | bytes 196640 | tf_op jit(solution)/shard_map/ppermute | solution.py:349
  186.7 1.1 fusion.1
  188.0 9.2 %collective-permute-done.8 = bf16[1024,128]{1,0:T(8,128)(2,1)S(1)} collective-permute-done((bf16[1024,128]{1,0:T(8,128)(2,1)S(1)}, bf16[1024,128]{1,0:T(8,128)(2,1)S(1)}, u32[]{:S(2)}, u32[]{:S(2)}) %collective-permute-start.8) | collective-permute-done | bytes 262176 | tf_op jit(solution)/shard_map/ppermute | solution.py:349
  (63 shorter events, 9.0 us)
Async XLA Ops:
  1.9 23.8 %collective-permute-start = (bf16[256,1024]{1,0:T(8,128)(2,1)}, bf16[256,1024]{1,0:T(8,128)(2,1)S(1)}, u32[]{:S(2)}, u32[]{:S(2)}) collective-permute-start(bf16[256,1024]{1,0:T(8,128)(2,1)} %take_tile.1), channel_id=1, source_target_pairs={{1,0},{2,1},{3,2},{4,3},{5,4},{6,5},{7,6},{8,7},{9,8},{10,9},{11,1... | collective-permute-start | bytes 1572872 | tf_op jit(solution)/shard_map/ppermute | solution.py:349
  3.2 12.4 %copy-start.18 = (s32[64,8]{0,1:T(8,128)S(1)}, s32[64,8]{0,1:T(8,128)}, u32[]{:S(2)}) copy-start(s32[64,8]{0,1:T(8,128)} %param.5) | copy-start | bytes 6148
  7.4 22.7 %collective-permute-start.1 = (bf16[128,2048]{1,0:T(8,128)(2,1)}, bf16[128,2048]{1,0:T(8,128)(2,1)S(1)}, u32[]{:S(2)}, u32[]{:S(2)}) collective-permute-start(bf16[128,2048]{1,0:T(8,128)(2,1)} %get-tuple-element.53), channel_id=1, source_target_pairs={{0,1},{1,0},{2,3},{3,2},{4,5},{5,4},{6,7},{7,6},{8,9},{9,8},{10,11... | collective-permute-start | bytes 1572872 | tf_op jit(solution)/shard_map/ppermute | solution.py:349
  12.2 17.9 %collective-permute-start.2 = (bf16[256,1024]{1,0:T(8,128)(2,1)S(1)}, bf16[256,1024]{1,0:T(8,128)(2,1)S(1)}, u32[]{:S(2)}, u32[]{:S(2)}) collective-permute-start(bf16[256,1024]{1,0:T(8,128)(2,1)S(1)} %get-tuple-element.55), channel_id=1, source_target_pairs={{0,2},{1,3},{2,4},{3,5},{4,6},{5,7},{6,8},{7,9},{8,10},{9,11},{10,... | collective-permute-start | bytes 1572872 | tf_op jit(solution)/shard_map/ppermute | solution.py:349
  14.3 15.8 %collective-permute-start.3 = (bf16[256,1024]{1,0:T(8,128)(2,1)S(1)}, bf16[256,1024]{1,0:T(8,128)(2,1)S(1)}, u32[]{:S(2)}, u32[]{:S(2)}) collective-permute-start(bf16[256,1024]{1,0:T(8,128)(2,1)S(1)} %get-tuple-element.56), channel_id=1, source_target_pairs={{2,0},{3,1},{4,2},{5,3},{6,4},{7,5},{8,6},{9,7},{10,8},{11,9},{12,... | collective-permute-start | bytes 1572872 | tf_op jit(solution)/shard_map/ppermute | solution.py:349
  25.6 19.4 %copy-start.17 = (bf16[256,1024]{1,0:T(8,128)(2,1)}, bf16[256,1024]{1,0:T(8,128)(2,1)S(1)}, u32[]{:S(2)}) copy-start(bf16[256,1024]{1,0:T(8,128)(2,1)S(1)} %collective-permute-done.m_ref) | copy-start | bytes 1572868
  30.1 14.9 %copy-start.3 = (bf16[128,2048]{1,0:T(8,128)(2,1)}, bf16[128,2048]{1,0:T(8,128)(2,1)S(1)}, u32[]{:S(2)}) copy-start(bf16[128,2048]{1,0:T(8,128)(2,1)S(1)} %collective-permute-done.1.refs_0_.refs_2_.refs_4_) | copy-start | bytes 1572868
  30.1 0.8 copy-start.14
  30.1 1.0 copy-start.15
  30.1 16.1 %copy-start.20 = (bf16[256,256]{1,0:T(8,128)(2,1)S(1)}, bf16[256,256]{1,0:T(8,128)(2,1)}, u32[]{:S(2)}) copy-start(bf16[256,256]{1,0:T(8,128)(2,1)} %get-tuple-element.57) | copy-start | bytes 393220
  30.1 35.6 %collective-permute-start.9 = (bf16[256,2048]{1,0:T(8,128)(2,1)}, bf16[256,2048]{1,0:T(8,128)(2,1)S(1)}, u32[]{:S(2)}, u32[]{:S(2)}) collective-permute-start(bf16[256,2048]{1,0:T(8,128)(2,1)} %get-tuple-element.67), channel_id=1, source_target_pairs={{0,1},{1,0},{2,3},{3,2},{4,5},{5,4},{6,7},{7,6},{8,9},{9,8},{10,11... | collective-permute-start | bytes 3145736 | tf_op jit(solution)/shard_map/ppermute | solution.py:349
  45.0 34.0 %collective-permute-start.10 = (bf16[256,2048]{1,0:T(8,128)(2,1)}, bf16[256,2048]{1,0:T(8,128)(2,1)S(1)}, u32[]{:S(2)}, u32[]{:S(2)}) collective-permute-start(bf16[256,2048]{1,0:T(8,128)(2,1)} %get-tuple-element.74), channel_id=1, source_target_pairs={{0,1},{1,0},{2,3},{3,2},{4,5},{5,4},{6,7},{7,6},{8,9},{9,8},{10,11... | collective-permute-start | bytes 3145736 | tf_op jit(solution)/shard_map/ppermute | solution.py:349
  46.2 3.5 %collective-permute-start.4 = (bf16[256,256]{1,0:T(8,128)(2,1)S(1)}, bf16[256,256]{1,0:T(8,128)(2,1)S(1)}, u32[]{:S(2)}, u32[]{:S(2)}) collective-permute-start(bf16[256,256]{1,0:T(8,128)(2,1)S(1)} %copy-done.20), channel_id=1, source_target_pairs={{2,0},{3,1},{4,2},{5,3},{6,4},{7,5},{8,6},{9,7},{10,8},{11,9},{12,... | collective-permute-start | bytes 393224 | tf_op jit(solution)/shard_map/ppermute | solution.py:349
  49.7 14.1 %copy-start.10 = (bf16[256,256]{1,0:T(8,128)(2,1)}, bf16[256,256]{1,0:T(8,128)(2,1)S(1)}, u32[]{:S(2)}) copy-start(bf16[256,256]{1,0:T(8,128)(2,1)S(1)} %collective-permute-done.4.refs_11_.refs_7_) | copy-start | bytes 393220
  65.8 1.0 copy-start.2
  79.0 18.9 %copy-start.1 = (bf16[256,2048]{1,0:T(8,128)(2,1)}, bf16[256,2048]{1,0:T(8,128)(2,1)S(1)}, u32[]{:S(2)}) copy-start(bf16[256,2048]{1,0:T(8,128)(2,1)S(1)} %collective-permute-done.10.refs_0_.refs_1_.refs_2_) | copy-start | bytes 3145732
  79.0 6.4 %collective-permute-start.11 = (bf16[2,4,384,128]{3,2,1,0:T(8,128)(2,1)}, bf16[2,4,384,128]{3,2,1,0:T(8,128)(2,1)S(1)}, u32[]{:S(2)}, u32[]{:S(2)}) collective-permute-start(bf16[2,4,384,128]{3,2,1,0:T(8,128)(2,1)} %get-tuple-element.75), channel_id=1, source_target_pairs={{0,2},{1,3},{2,0},{3,1},{4,6},{5,7},{6,4},{7,5},{8,10},{9,11},{10,... | collective-permute-start | bytes 2359304 | tf_op jit(solution)/shard_map/ppermute | solution.py:349
  82.9 11.9 %collective-permute-start.5 = (bf16[4,1024,128]{2,1,0:T(8,128)(2,1)}, bf16[4,1024,128]{2,1,0:T(8,128)(2,1)}, u32[]{:S(2)}, u32[]{:S(2)}) collective-permute-start(bf16[4,1024,128]{2,1,0:T(8,128)(2,1)} %get-tuple-element.60), channel_id=1, source_target_pairs={{0,2},{1,3},{2,0},{3,1},{4,6},{5,7},{6,4},{7,5},{8,10},{9,11},{10,... | collective-permute-start | bytes 3145736 | tf_op jit(solution)/shard_map/ppermute | solution.py:349
  83.0 46.6 %collective-permute-start.13 = (bf16[384,2048]{1,0:T(8,128)(2,1)}, bf16[384,2048]{1,0:T(8,128)(2,1)S(1)}, u32[]{:S(2)}, u32[]{:S(2)}) collective-permute-start(bf16[384,2048]{1,0:T(8,128)(2,1)} %get-tuple-element.81), channel_id=1, source_target_pairs={{0,1},{1,0},{2,3},{3,2},{4,5},{5,4},{6,7},{7,6},{8,9},{9,8},{10,11... | collective-permute-start | bytes 4718600 | tf_op jit(solution)/shard_map/ppermute | solution.py:349
  85.4 1.0 copy-start.12
  89.4 26.1 %all-to-all-start = ((bf16[8,384,128]{2,1,0:T(8,128)(2,1)}), bf16[8,384,128]{2,1,0:T(8,128)(2,1)S(1)}, u32[]{:S(2)}, u32[]{:S(2)}) async-start(bf16[8,384,128]{2,1,0:T(8,128)(2,1)} %bitcast.33), calls=%async_computation | async-start | bytes 1572864 | tf_op jit(solution)/shard_map/all_to_all | solution.py:427
  107.6 2.1 %collective-permute-start.12 = (bf16[2,4,256,128]{3,2,1,0:T(8,128)(2,1)}, bf16[2,4,256,128]{3,2,1,0:T(8,128)(2,1)S(1)}, u32[]{:S(2)}, u32[]{:S(2)}) collective-permute-start(bf16[2,4,256,128]{3,2,1,0:T(8,128)(2,1)} %get-tuple-element.79), channel_id=1, source_target_pairs={{0,2},{1,3},{2,0},{3,1},{4,6},{5,7},{6,4},{7,5},{8,10},{9,11},{10,... | collective-permute-start | bytes 1572872 | tf_op jit(solution)/shard_map/ppermute | solution.py:349
  107.6 18.8 %collective-permute-start.6 = (bf16[2,1024,128]{2,1,0:T(8,128)(2,1)}, bf16[2,1024,128]{2,1,0:T(8,128)(2,1)S(1)}, u32[]{:S(2)}, u32[]{:S(2)}) collective-permute-start(bf16[2,1024,128]{2,1,0:T(8,128)(2,1)} %get-tuple-element.62), channel_id=1, source_target_pairs={{0,4},{1,5},{2,6},{3,7},{4,0},{5,1},{6,2},{7,3},{8,12},{9,13},{10,... | collective-permute-start | bytes 1572872 | tf_op jit(solution)/shard_map/ppermute | solution.py:349
  109.7 0.8 copy-start.16
  115.5 27.0 %copy-start.4 = (bf16[8,384,128]{2,1,0:T(8,128)(2,1)}, bf16[8,384,128]{2,1,0:T(8,128)(2,1)S(1)}, u32[]{:S(2)}) copy-start(bf16[8,384,128]{2,1,0:T(8,128)(2,1)S(1)} %all-to-all-done.came_ref) | copy-start | bytes 2359300
  115.5 35.6 %all-to-all-start.1 = ((bf16[8,256,128]{2,1,0:T(8,128)(2,1)}), bf16[8,256,128]{2,1,0:T(8,128)(2,1)S(1)}, u32[]{:S(2)}, u32[]{:S(2)}) async-start(bf16[8,256,128]{2,1,0:T(8,128)(2,1)} %bitcast.35), calls=%async_computation.1 | async-start | bytes 1048576 | tf_op jit(solution)/shard_map/all_to_all | solution.py:427
  126.5 0.8 copy-start.8
  129.6 1.2 copy-start
  144.4 12.4 %copy-start.9 = (f32[384,128]{1,0:T(8,128)S(1)}, f32[384,128]{1,0:T(8,128)}, u32[]{:S(2)}) copy-start(f32[384,128]{1,0:T(8,128)} %gather_up_sums.3) | copy-start | bytes 589828
  144.4 18.6 %copy-start.19 = (bf16[1,1024,128]{2,1,0:T(8,128)(2,1)S(1)}, bf16[1,1024,128]{2,1,0:T(8,128)(2,1)}, u32[]{:S(2)}) copy-start(bf16[1,1024,128]{2,1,0:T(8,128)(2,1)} %get-tuple-element.64) | copy-start | bytes 786436
  144.4 2.5 %collective-permute-start.14 = (bf16[2,4,384,128]{3,2,1,0:T(8,128)(2,1)}, bf16[2,4,384,128]{3,2,1,0:T(8,128)(2,1)S(1)}, u32[]{:S(2)}, u32[]{:S(2)}) collective-permute-start(bf16[2,4,384,128]{3,2,1,0:T(8,128)(2,1)} %get-tuple-element.86), channel_id=1, source_target_pairs={{0,2},{1,3},{2,0},{3,1},{4,6},{5,7},{6,4},{7,5},{8,10},{9,11},{10,... | collective-permute-start | bytes 2359304 | tf_op jit(solution)/shard_map/ppermute | solution.py:349
  146.9 0.9 copy-start.13
  147.8 35.2 %copy-start.6 = (f32[1,1024,128]{2,1,0:T(8,128)S(1)}, f32[1,1024,128]{2,1,0:T(8,128)}, u32[]{:S(2)}) copy-start(f32[1,1024,128]{2,1,0:T(8,128)} %get-tuple-element.63) | copy-start | bytes 1572868
  151.1 0.8 copy-start.7
  151.9 25.5 %all-to-all-start.2 = ((bf16[8,384,128]{2,1,0:T(8,128)(2,1)}), bf16[8,384,128]{2,1,0:T(8,128)(2,1)S(1)}, u32[]{:S(2)}, u32[]{:S(2)}) async-start(bf16[8,384,128]{2,1,0:T(8,128)(2,1)} %bitcast.34), calls=%async_computation.2 | async-start | bytes 1572864 | tf_op jit(solution)/shard_map/all_to_all | solution.py:427
  158.8 27.8 %copy-start.11 = (f32[256,128]{1,0:T(8,128)S(1)}, f32[256,128]{1,0:T(8,128)}, u32[]{:S(2)}) copy-start(f32[256,128]{1,0:T(8,128)} %gather_up_sums.4) | copy-start | bytes 393220
  160.2 20.0 %collective-permute-start.15 = (f32[8,80,128]{1,2,0:T(8,128)S(1)}, f32[8,80,128]{1,2,0:T(8,128)S(1)}, u32[]{:S(2)}, u32[]{:S(2)}) collective-permute-start(f32[8,80,128]{1,2,0:T(8,128)S(1)} %pad_maximum_fusion), channel_id=1, source_target_pairs={{0,1},{2,3},{4,5},{6,7},{8,9},{10,11},{12,13},{14,15},{17,16},{19,... | collective-permute-start | bytes 983048 | tf_op jit(solution)/shard_map/ppermute | solution.py:349
  163.0 20.0 %collective-permute-start.7 = (bf16[1,1024,128]{2,1,0:T(8,128)(2,1)S(1)}, bf16[1,1024,128]{2,1,0:T(8,128)(2,1)S(1)}, u32[]{:S(2)}, u32[]{:S(2)}) collective-permute-start(bf16[1,1024,128]{2,1,0:T(8,128)(2,1)S(1)} %copy-done.19), channel_id=1, source_target_pairs={{0,8},{1,9},{2,10},{3,11},{4,12},{5,13},{6,14},{7,15},{8,0},{9,1},... | collective-permute-start | bytes 786440 | tf_op jit(solution)/shard_map/ppermute | solution.py:349
  177.4 0.9 copy-start.5
  180.2 6.2 %collective-permute-start.16 = (f32[8,48,128]{2,1,0:T(8,128)}, f32[8,48,128]{2,1,0:T(8,128)S(1)}, u32[]{:S(2)}, u32[]{:S(2)}) collective-permute-start(f32[8,48,128]{2,1,0:T(8,128)} %bitcast.42), channel_id=1, source_target_pairs={{0,1},{2,3},{4,5},{6,7},{8,9},{10,11},{12,13},{14,15},{17,16},{19,... | collective-permute-start | bytes 589832 | tf_op jit(solution)/shard_map/ppermute | solution.py:349
  183.1 14.2 %collective-permute-start.8 = (bf16[1024,128]{1,0:T(8,128)(2,1)S(1)}, bf16[1024,128]{1,0:T(8,128)(2,1)S(1)}, u32[]{:S(2)}, u32[]{:S(2)}) collective-permute-start(bf16[1024,128]{1,0:T(8,128)(2,1)S(1)} %bitcast_convert_fusion), channel_id=1, source_target_pairs={{1,17},{3,19},{5,21},{7,23},{9,25},{11,27},{13,29},{15,31},{16,0},... | collective-permute-start | bytes 786440 | tf_op jit(solution)/shard_map/ppermute | solution.py:349
where the time goes:
time: 199 us; the launch traced here: 198 us
  Pallas kernels  99.2 us (50%)
  waiting for transfers between devices  42.5 us (21%)
  starting transfers between devices  40.7 us (20%)
  local copies, waits for them, and re-layouts  12 us (6%)
  other arithmetic  3.45 us (2%)
    pallas_call x3, Pallas kernels, pair_products(): pl.pallas_call(functools.partial(pair_kernel, steps, cols, widths), grid_...  33.7 us
    ppermute x17, waiting for transfers between devices, send(): return lax.ppermute(value, AXES, flat)  28 us
    ppermute x17, starting transfers between devices, send(): return lax.ppermute(value, AXES, flat)  26.5 us
    all_to_all x3, waiting for transfers between devices, deal_out(): return lax.all_to_all(parts, 'slab', 0, 0, axis_index_groups=same_core)  14.5 us
    all_to_all x3, starting transfers between devices, deal_out(): return lax.all_to_all(parts, 'slab', 0, 0, axis_index_groups=same_core)  14.2 us
    pallas_call x1, Pallas kernels, own_square(): pl.pallas_call(functools.partial(square_kernel, steps, cols), grid_spec=p...  14.1 us
    pallas_call x1, Pallas kernels, own_kphi(): pl.pallas_call(functools.partial(kphi_kernel, steps), grid=(steps,), in_s...  13.9 us
    pallas_call x1, Pallas kernels, expand(): pl.pallas_call(functools.partial(expand_kernel, count), grid_spec=pltpu.P...  9.35 us
  transfers between devices with their start and end apart: 20, of which 9 were waited for; matrix products, arithmetic and copies ran while one was open for 3% of the time, Pallas kernels for 49%

commit v1 on v0

--- a/solution.py
+++ b/solution.py
@@ -19,7 +19,7 @@
 BF16 = jnp.bfloat16
 NT = (((1,), (1,)), ((), ()))
 TN = (((0,), (0,)), ((), ()))
-VMEM_LIMIT = 56 * 1024 * 1024
+VMEM_LIMIT = 62 * 1024 * 1024
 
 
 def dot(a, b, dims=(((1,), (0,)), ((), ()))):

time: 199 us -> 196 us (0.985)
  waiting for transfers between devices: 42.5 us -> 38.8 us
  local copies, waits for them, and re-layouts: 12 us -> 8.52 us
  starting transfers between devices: 40.7 us -> 43.5 us
    unnamed x43 -> x25, local copies, waits for them, and re-layouts: 8.95 us -> 4.59 us
    ppermute x17, waiting for transfers between devices: 28 us -> 25.4 us  [send(): return lax.ppermute(value, AXES, flat)]
    ppermute x17, starting transfers between devices: 26.5 us -> 28.5 us  [send(): return lax.ppermute(value, AXES, flat)]
  transfers between devices with their start and end apart: 20 -> 20, of which waited for: 9 -> 10; matrix products, arithmetic and copies ran while one was open for 3% -> 4% of each run, Pallas kernels for 49% -> 50%
where the time goes in v1:
time: 196 us; the launch traced here: 195 us
  Pallas kernels  99.4 us (51%)
  starting transfers between devices  43.5 us (22%)
  waiting for transfers between devices  38.8 us (20%)
  local copies, waits for them, and re-layouts  8.52 us (4%)
  other arithmetic  4.68 us (2%)
    pallas_call x3, Pallas kernels, pair_products(): pl.pallas_call(functools.partial(pair_kernel, steps, cols, widths), grid_...  33.7 us
    ppermute x17, starting transfers between devices, send(): return lax.ppermute(value, AXES, flat)  28.5 us
    ppermute x17, waiting for transfers between devices, send(): return lax.ppermute(value, AXES, flat)  25.4 us
    all_to_all x3, starting transfers between devices, deal_out(): return lax.all_to_all(parts, 'slab', 0, 0, axis_index_groups=same_core)  15 us
    pallas_call x1, Pallas kernels, own_square(): pl.pallas_call(functools.partial(square_kernel, steps, cols), grid_spec=p...  14.1 us
    pallas_call x1, Pallas kernels, own_kphi(): pl.pallas_call(functools.partial(kphi_kernel, steps), grid=(steps,), in_s...  14 us
    all_to_all x3, waiting for transfers between devices, deal_out(): return lax.all_to_all(parts, 'slab', 0, 0, axis_index_groups=same_core)  13.4 us
    pallas_call x1, Pallas kernels, expand(): pl.pallas_call(functools.partial(expand_kernel, count), grid_spec=pltpu.P...  9.36 us
  transfers between devices with their start and end apart: 20, of which 10 were waited for; matrix products, arithmetic and copies ran while one was open for 4% of the time, Pallas kernels for 50%

profile of v1, /device:TPU:0, one launch (start us, length us, event | category | flops | bytes accessed | tf_op | source)
XLA Modules:
  0.0 195.1 jit_solution(11366183459333073375)
XLA Ops:
  0.0 1.9 take_tile.1
  1.9 1.3 collective-permute-start
  3.2 4.2 %turn.2 = (bf16[128,2048]{1,0:T(8,128)(2,1)}, bf16[256,2048]{1,0:T(8,128)(2,1)}, bf16[256,2048]{1,0:T(8,128)(2,1)}, bf16[384,2048]{1,0:T(8,128)(2,1)}) custom-call(s32[1]{0:T(128)} %bitcast.3.at_ref, bf16[4096,1024]{1,0:T(8,128)(2,1)} %refs_8_.5), custom_call_target="tpu_custom_call" | custom-call | tf_op jit(solution)/shard_map/turn/pallas_call | solution.py:177
  7.4 3.6 %collective-permute-start.1 = (bf16[128,2048]{1,0:T(8,128)(2,1)}, bf16[128,2048]{1,0:T(8,128)(2,1)S(1)}, u32[]{:S(2)}, u32[]{:S(2)}) collective-permute-start(bf16[128,2048]{1,0:T(8,128)(2,1)} %get-tuple-element.53), channel_id=1, source_target_pairs={{0,1},{1,0},{2,3},{3,2},{4,5},{5,4},{6,7},{7,6},{8,9},{9,8},{10,11... | collective-permute-start | bytes 1572872 | tf_op jit(solution)/shard_map/ppermute | solution.py:349
  11.0 2.2 %fusion.2 = (bf16[256,1024]{1,0:T(8,128)(2,1)}, bf16[256,1024]{1,0:T(8,128)(2,1)}) fusion(bf16[4096,1024]{1,0:T(8,128)(2,1)} %refs_8_.5), kind=kLoop, calls=%fused_computation.11 | loop fusion | bytes 2097152 | tf_op jit(solution)/shard_map/slice | solution.py:391
  13.3 2.0 %collective-permute-start.2 = (bf16[256,1024]{1,0:T(8,128)(2,1)}, bf16[256,1024]{1,0:T(8,128)(2,1)S(1)}, u32[]{:S(2)}, u32[]{:S(2)}) collective-permute-start(bf16[256,1024]{1,0:T(8,128)(2,1)} %get-tuple-element.55), channel_id=1, source_target_pairs={{0,2},{1,3},{2,4},{3,5},{4,6},{5,7},{6,8},{7,9},{8,10},{9,11},{10,... | collective-permute-start | bytes 1572872 | tf_op jit(solution)/shard_map/ppermute | solution.py:349
  15.3 1.3 collective-permute-start.3
  17.3 9.4 %expand_band.1 = (bf16[16,256,768]{2,1,0:T(8,128)(2,1)}, bf16[256,256]{1,0:T(8,128)(2,1)}) custom-call(s32[64,8]{1,0:T(8,128)} %copy.4.off_ref, bf16[4096,512]{1,0:T(8,128)(2,1)} %k_ref), custom_call_target="tpu_custom_call" | custom-call | tf_op jit(solution)/shard_map/expand_band/pallas_call | solution.py:66
  26.7 3.4 %collective-permute-done.1.refs_0_.refs_2_.refs_4_ = bf16[128,2048]{1,0:T(8,128)(2,1)S(1)} collective-permute-done((bf16[128,2048]{1,0:T(8,128)(2,1)}, bf16[128,2048]{1,0:T(8,128)(2,1)S(1)}, u32[]{:S(2)}, u32[]{:S(2)}) %collective-permute-start.1) | collective-permute-done | bytes 524320 | tf_op jit(solution)/shard_map/ppermute | solution.py:349
  31.1 14.0 %own_kphi.1.z_ref.refs_9_.refs_5_ = bf16[4096,1024]{1,0:T(8,128)(2,1)} custom-call(bf16[16,256,768]{2,1,0:T(8,128)(2,1)} %get-tuple-element.54.kb_ref.refs_10_.refs_6_, bf16[4096,1024]{1,0:T(8,128)(2,1)} %refs_8_.5, bf16[4096,1024]{1,0:T(8,128)(2,1)} %refs_8_.5, bf16[4096,1024]{1,0:T(8,128)(2,1)} %refs_8_.5, bf16[256,1024]{1,0:T(8,128)(2,1)} %copy-done.8, ...), custom_call_target="tpu_custom_call" | custom-call | tf_op jit(solution)/shard_map/own_kphi/pallas_call | solution.py:212
  45.1 1.1 collective-permute-start.10
  46.2 1.3 collective-permute-start.4
  48.2 1.5 collective-permute-done.4.refs_11_.refs_7_
  49.7 14.1 %own_square.1 = (f32[4,1024,128]{2,1,0:T(8,128)}, bf16[4,1024,128]{2,1,0:T(8,128)(2,1)}) custom-call(s32[1]{0:T(128)} %bitcast.2.at_ref, bf16[4096,1024]{1,0:T(8,128)(2,1)} %refs_8_.5, bf16[4096,1024]{1,0:T(8,128)(2,1)} %own_kphi.1.z_ref.refs_9_.refs_5_), custom_call_target="tpu_custom_call" | custom-call | tf_op jit(solution)/shard_map/own_square/pallas_call | solution.py:252
  63.7 2.0 %turn.3 = (bf16[128,256]{1,0:T(8,128)(2,1)}, bf16[256,256]{1,0:T(8,128)(2,1)}, bf16[256,256]{1,0:T(8,128)(2,1)}, bf16[384,256]{1,0:T(8,128)(2,1)}) custom-call(s32[1]{0:T(128)} %constant.78.clone.1.at_ref, bf16[256,1024]{1,0:T(8,128)(2,1)} %collective-permute-done.m_ref), custom_call_target="tpu_custom_call" | custom-call | tf_op jit(solution)/shard_map/turn/pallas_call | solution.py:177
  65.7 12.3 %pair_products.3 = (f32[2,4,384,128]{3,2,1,0:T(8,128)}, bf16[2,4,384,128]{3,2,1,0:T(8,128)(2,1)}) custom-call(s32[2]{0:T(128)} %pad_add_fusion.1.at_ref, bf16[16,256,768]{2,1,0:T(8,128)(2,1)} %get-tuple-element.54.kb_ref.refs_10_.refs_6_, bf16[128,2048]{1,0:T(8,128)(2,1)} %copy-done.2, bf16[256,2048]{1,0:T(8,128)(2,1)} %collective-permute-done.9.refs_1_.refs_3_.refs_5_, ...), custom_call_target="tpu_custom_call" | custom-call | tf_op jit(solution)/shard_map/pair_products/pallas_call | solution.py:314
  78.3 3.7 %collective-permute-start.11 = (bf16[2,4,384,128]{3,2,1,0:T(8,128)(2,1)}, bf16[2,4,384,128]{3,2,1,0:T(8,128)(2,1)}, u32[]{:S(2)}, u32[]{:S(2)}) collective-permute-start(bf16[2,4,384,128]{3,2,1,0:T(8,128)(2,1)} %get-tuple-element.75), channel_id=1, source_target_pairs={{0,2},{1,3},{2,0},{3,1},{4,6},{5,7},{6,4},{7,5},{8,10},{9,11},{10,... | collective-permute-start | bytes 2359304 | tf_op jit(solution)/shard_map/ppermute | solution.py:349
  82.1 0.9 collective-permute-start.5
  84.5 3.2 %deal_out_sums.3 = bf16[2,4,384,128]{3,2,1,0:T(8,128)(2,1)} custom-call(s32[2]{0:T(128)} %pad_add_fusion.at_ref, f32[2,4,384,128]{3,2,1,0:T(8,128)} %get-tuple-element.71.mine_ref, bf16[2,4,384,128]{3,2,1,0:T(8,128)(2,1)} %collective-permute-done.11.came_ref), custom_call_target="tpu_custom_call" | custom-call | tf_op jit(solution)/shard_map/deal_out_sums/pallas_call | solution.py:136
  87.7 5.3 %all-to-all-start = ((bf16[8,384,128]{2,1,0:T(8,128)(2,1)}), bf16[8,384,128]{2,1,0:T(8,128)(2,1)}, u32[]{:S(2)}, u32[]{:S(2)}) async-start(bf16[8,384,128]{2,1,0:T(8,128)(2,1)} %bitcast.33), calls=%async_computation | async-start | bytes 1572864 | tf_op jit(solution)/shard_map/all_to_all | solution.py:427
  93.0 3.1 %fold.2 = (f32[2,1024,128]{2,1,0:T(8,128)}, bf16[2,1024,128]{2,1,0:T(8,128)(2,1)}) custom-call(s32[1]{0:T(128)} %bitcast.1.at_ref, f32[2,2,1024,128]{3,2,1,0:T(8,128)} %bitcast.29, bf16[2,2,1024,128]{3,2,1,0:T(8,128)(2,1)} %bitcast.6.came_keep_ref.came_give_ref, f32[2,2,1024,128]{3,2,1,0:T(8,128)} %bitcast.30, ...), custom_call_target="tpu_custom_call" | custom-call | tf_op jit(solution)/shard_map/fold/pallas_call | solution.py:115
  96.1 9.6 %pair_products.4 = (f32[2,4,256,128]{3,2,1,0:T(8,128)}, bf16[2,4,256,128]{3,2,1,0:T(8,128)(2,1)}) custom-call(s32[2]{0:T(128)} %pad_add_fusion.1.at_ref, bf16[16,256,768]{2,1,0:T(8,128)(2,1)} %get-tuple-element.54.kb_ref.refs_10_.refs_6_, bf16[256,2048]{1,0:T(8,128)(2,1)} %copy-done.1, bf16[256,2048]{1,0:T(8,128)(2,1)} %copy-done.1, ...), custom_call_target="tpu_custom_call" | custom-call | tf_op jit(solution)/shard_map/pair_products/pallas_call | solution.py:314
  105.7 2.1 %collective-permute-start.6 = (bf16[2,1024,128]{2,1,0:T(8,128)(2,1)}, bf16[2,1024,128]{2,1,0:T(8,128)(2,1)}, u32[]{:S(2)}, u32[]{:S(2)}) collective-permute-start(bf16[2,1024,128]{2,1,0:T(8,128)(2,1)} %get-tuple-element.62), channel_id=1, source_target_pairs={{0,4},{1,5},{2,6},{3,7},{4,0},{5,1},{6,2},{7,3},{8,12},{9,13},{10,... | collective-permute-start | bytes 1572872 | tf_op jit(solution)/shard_map/ppermute | solution.py:349
  108.0 2.8 %deal_out_sums.4 = bf16[2,4,256,128]{3,2,1,0:T(8,128)(2,1)} custom-call(s32[2]{0:T(128)} %pad_add_fusion.at_ref, f32[2,4,256,128]{3,2,1,0:T(8,128)} %get-tuple-element.78.mine_ref, bf16[2,4,256,128]{3,2,1,0:T(8,128)(2,1)} %collective-permute-done.12.came_ref), custom_call_target="tpu_custom_call" | custom-call | tf_op jit(solution)/shard_map/deal_out_sums/pallas_call | solution.py:136
  110.7 2.8 %all-to-all-done.came_ref = bf16[8,384,128]{2,1,0:T(8,128)(2,1)} async-done(((bf16[8,384,128]{2,1,0:T(8,128)(2,1)}), bf16[8,384,128]{2,1,0:T(8,128)(2,1)}, u32[]{:S(2)}, u32[]{:S(2)}) %all-to-all-start) | async-done | bytes 786464 | tf_op jit(solution)/shard_map/all_to_all | solution.py:427
  113.6 4.1 %all-to-all-start.1 = ((bf16[8,256,128]{2,1,0:T(8,128)(2,1)}), bf16[8,256,128]{2,1,0:T(8,128)(2,1)}, u32[]{:S(2)}, u32[]{:S(2)}) async-start(bf16[8,256,128]{2,1,0:T(8,128)(2,1)} %bitcast.35), calls=%async_computation.1 | async-start | bytes 1048576 | tf_op jit(solution)/shard_map/all_to_all | solution.py:427
  117.7 6.5 %collective-permute-done.6 = bf16[2,1024,128]{2,1,0:T(8,128)(2,1)} collective-permute-done((bf16[2,1024,128]{2,1,0:T(8,128)(2,1)}, bf16[2,1024,128]{2,1,0:T(8,128)(2,1)}, u32[]{:S(2)}, u32[]{:S(2)}) %collective-permute-start.6) | collective-permute-done | bytes 524320 | tf_op jit(solution)/shard_map/ppermute | solution.py:349
  124.2 2.3 %fold.3 = (f32[1,1024,128]{2,1,0:T(8,128)}, bf16[1,1024,128]{2,1,0:T(8,128)(2,1)}) custom-call(s32[1]{0:T(128)} %bitcast.at_ref, f32[1,2,1024,128]{3,2,1,0:T(8,128)} %bitcast.31, bf16[1,2,1024,128]{3,2,1,0:T(8,128)(2,1)} %bitcast.8.came_keep_ref.came_give_ref, f32[1,2,1024,128]{3,2,1,0:T(8,128)} %bitcast.32, ...), custom_call_target="tpu_custom_call" | custom-call | tf_op jit(solution)/shard_map/fold/pallas_call | solution.py:115
  126.5 1.2 copy-done
  127.7 11.8 %pair_products.5 = (f32[2,4,384,128]{3,2,1,0:T(8,128)}, bf16[2,4,384,128]{3,2,1,0:T(8,128)(2,1)}) custom-call(s32[2]{0:T(128)} %pad_add_fusion.1.at_ref, bf16[16,256,768]{2,1,0:T(8,128)(2,1)} %get-tuple-element.54.kb_ref.refs_10_.refs_6_, bf16[384,2048]{1,0:T(8,128)(2,1)} %copy-done, bf16[384,2048]{1,0:T(8,128)(2,1)} %copy-done, bf16[384,2048]{1,0:T(8,128)(2,1)} %copy-done, ...), custom_call_target="tpu_custom_call" | custom-call | tf_op jit(solution)/shard_map/pair_products/pallas_call | solution.py:314
  139.4 1.9 gather_up_sums.3
  141.3 2.5 %collective-permute-done.14.came_ref = bf16[2,4,384,128]{3,2,1,0:T(8,128)(2,1)S(1)} collective-permute-done((bf16[2,4,384,128]{3,2,1,0:T(8,128)(2,1)}, bf16[2,4,384,128]{3,2,1,0:T(8,128)(2,1)S(1)}, u32[]{:S(2)}, u32[]{:S(2)}) %collective-permute-start.14) | collective-permute-done | bytes 786464 | tf_op jit(solution)/shard_map/ppermute | solution.py:349
  143.8 0.9 copy-done.7
  144.7 3.3 %deal_out_sums.5 = bf16[2,4,384,128]{3,2,1,0:T(8,128)(2,1)} custom-call(s32[2]{0:T(128)} %pad_add_fusion.at_ref, f32[2,4,384,128]{3,2,1,0:T(8,128)} %get-tuple-element.84.mine_ref, bf16[2,4,384,128]{3,2,1,0:T(8,128)(2,1)} %copy-done.7), custom_call_target="tpu_custom_call" | custom-call | tf_op jit(solution)/shard_map/deal_out_sums/pallas_call | solution.py:136
  148.0 5.6 %all-to-all-start.2 = ((bf16[8,384,128]{2,1,0:T(8,128)(2,1)}), bf16[8,384,128]{2,1,0:T(8,128)(2,1)S(1)}, u32[]{:S(2)}, u32[]{:S(2)}) async-start(bf16[8,384,128]{2,1,0:T(8,128)(2,1)} %bitcast.34), calls=%async_computation.2 | async-start | bytes 1572864 | tf_op jit(solution)/shard_map/all_to_all | solution.py:427
  153.8 1.8 gather_up_sums.4
  155.5 1.1 copy.6
  156.7 1.0 pad_maximum_fusion
  157.7 3.9 %collective-permute-start.15 = (f32[8,80,128]{1,2,0:T(8,128)}, f32[8,80,128]{1,2,0:T(8,128)}, u32[]{:S(2)}, u32[]{:S(2)}) collective-permute-start(f32[8,80,128]{1,2,0:T(8,128)} %pad_maximum_fusion), channel_id=1, source_target_pairs={{0,1},{2,3},{4,5},{6,7},{8,9},{10,11},{12,13},{14,15},{17,16},{19,... | collective-permute-start | bytes 983048 | tf_op jit(solution)/shard_map/ppermute | solution.py:349
  161.5 2.0 %collective-permute-start.7 = (bf16[1,1024,128]{2,1,0:T(8,128)(2,1)}, bf16[1,1024,128]{2,1,0:T(8,128)(2,1)S(1)}, u32[]{:S(2)}, u32[]{:S(2)}) collective-permute-start(bf16[1,1024,128]{2,1,0:T(8,128)(2,1)} %get-tuple-element.64), channel_id=1, source_target_pairs={{0,8},{1,9},{2,10},{3,11},{4,12},{5,13},{6,14},{7,15},{8,0},{9,1},... | collective-permute-start | bytes 786440 | tf_op jit(solution)/shard_map/ppermute | solution.py:349
  163.5 10.6 %all-to-all-done.2.came_ref = bf16[8,384,128]{2,1,0:T(8,128)(2,1)S(1)} async-done(((bf16[8,384,128]{2,1,0:T(8,128)(2,1)}), bf16[8,384,128]{2,1,0:T(8,128)(2,1)S(1)}, u32[]{:S(2)}, u32[]{:S(2)}) %all-to-all-start.2) | async-done | bytes 786464 | tf_op jit(solution)/shard_map/all_to_all | solution.py:427
  174.1 0.9 copy-done.3
  175.0 1.9 gather_up_sums.5
  176.9 3.1 %collective-permute-start.16 = (f32[8,48,128]{2,1,0:T(8,128)}, f32[8,48,128]{2,1,0:T(8,128)S(1)}, u32[]{:S(2)}, u32[]{:S(2)}) collective-permute-start(f32[8,48,128]{2,1,0:T(8,128)} %bitcast.40), channel_id=1, source_target_pairs={{0,1},{2,3},{4,5},{6,7},{8,9},{10,11},{12,13},{14,15},{17,16},{19,... | collective-permute-start | bytes 589832 | tf_op jit(solution)/shard_map/ppermute | solution.py:349
  180.1 1.3 collective-permute-start.8
  181.4 2.1 %collective-permute-done.16 = f32[8,48,128]{2,1,0:T(8,128)S(1)} collective-permute-done((f32[8,48,128]{2,1,0:T(8,128)}, f32[8,48,128]{2,1,0:T(8,128)S(1)}, u32[]{:S(2)}, u32[]{:S(2)}) %collective-permute-start.16) | collective-permute-done | bytes 196640 | tf_op jit(solution)/shard_map/ppermute | solution.py:349
  183.7 1.4 fusion.1
  185.3 8.9 %collective-permute-done.8 = bf16[1024,128]{1,0:T(8,128)(2,1)S(1)} collective-permute-done((bf16[1024,128]{1,0:T(8,128)(2,1)S(1)}, bf16[1024,128]{1,0:T(8,128)(2,1)S(1)}, u32[]{:S(2)}, u32[]{:S(2)}) %collective-permute-start.8) | collective-permute-done | bytes 262176 | tf_op jit(solution)/shard_map/ppermute | solution.py:349
  (45 shorter events, 5.9 us)
Async XLA Ops:
  1.9 24.8 %collective-permute-start = (bf16[256,1024]{1,0:T(8,128)(2,1)}, bf16[256,1024]{1,0:T(8,128)(2,1)}, u32[]{:S(2)}, u32[]{:S(2)}) collective-permute-start(bf16[256,1024]{1,0:T(8,128)(2,1)} %take_tile.1), channel_id=1, source_target_pairs={{1,0},{2,1},{3,2},{4,3},{5,4},{6,5},{7,6},{8,7},{9,8},{10,9},{11,1... | collective-permute-start | bytes 1572872 | tf_op jit(solution)/shard_map/ppermute | solution.py:349
  3.2 13.4 %copy-start.10 = (s32[64,8]{0,1:T(8,128)S(1)}, s32[64,8]{0,1:T(8,128)}, u32[]{:S(2)}) copy-start(s32[64,8]{0,1:T(8,128)} %param.5) | copy-start | bytes 6148
  7.4 22.7 %collective-permute-start.1 = (bf16[128,2048]{1,0:T(8,128)(2,1)}, bf16[128,2048]{1,0:T(8,128)(2,1)S(1)}, u32[]{:S(2)}, u32[]{:S(2)}) collective-permute-start(bf16[128,2048]{1,0:T(8,128)(2,1)} %get-tuple-element.53), channel_id=1, source_target_pairs={{0,1},{1,0},{2,3},{3,2},{4,5},{5,4},{6,7},{7,6},{8,9},{9,8},{10,11... | collective-permute-start | bytes 1572872 | tf_op jit(solution)/shard_map/ppermute | solution.py:349
  13.3 16.9 %collective-permute-start.2 = (bf16[256,1024]{1,0:T(8,128)(2,1)}, bf16[256,1024]{1,0:T(8,128)(2,1)S(1)}, u32[]{:S(2)}, u32[]{:S(2)}) collective-permute-start(bf16[256,1024]{1,0:T(8,128)(2,1)} %get-tuple-element.55), channel_id=1, source_target_pairs={{0,2},{1,3},{2,4},{3,5},{4,6},{5,7},{6,8},{7,9},{8,10},{9,11},{10,... | collective-permute-start | bytes 1572872 | tf_op jit(solution)/shard_map/ppermute | solution.py:349
  15.3 14.8 %collective-permute-start.3 = (bf16[256,1024]{1,0:T(8,128)(2,1)}, bf16[256,1024]{1,0:T(8,128)(2,1)S(1)}, u32[]{:S(2)}, u32[]{:S(2)}) collective-permute-start(bf16[256,1024]{1,0:T(8,128)(2,1)} %get-tuple-element.56), channel_id=1, source_target_pairs={{2,0},{3,1},{4,2},{5,3},{6,4},{7,5},{8,6},{9,7},{10,8},{11,9},{12,... | collective-permute-start | bytes 1572872 | tf_op jit(solution)/shard_map/ppermute | solution.py:349
  30.1 15.0 %copy-start.2 = (bf16[128,2048]{1,0:T(8,128)(2,1)}, bf16[128,2048]{1,0:T(8,128)(2,1)S(1)}, u32[]{:S(2)}) copy-start(bf16[128,2048]{1,0:T(8,128)(2,1)S(1)} %collective-permute-done.1.refs_0_.refs_2_.refs_4_) | copy-start | bytes 1572868
  30.1 0.8 copy-start.8
  30.1 1.0 copy-start.9
  30.1 16.1 %copy-start.11 = (bf16[256,256]{1,0:T(8,128)(2,1)S(1)}, bf16[256,256]{1,0:T(8,128)(2,1)}, u32[]{:S(2)}) copy-start(bf16[256,256]{1,0:T(8,128)(2,1)} %get-tuple-element.57) | copy-start | bytes 393220
  30.2 35.6 %collective-permute-start.9 = (bf16[256,2048]{1,0:T(8,128)(2,1)}, bf16[256,2048]{1,0:T(8,128)(2,1)}, u32[]{:S(2)}, u32[]{:S(2)}) collective-permute-start(bf16[256,2048]{1,0:T(8,128)(2,1)} %get-tuple-element.67), channel_id=1, source_target_pairs={{0,1},{1,0},{2,3},{3,2},{4,5},{5,4},{6,7},{7,6},{8,9},{9,8},{10,11... | collective-permute-start | bytes 3145736 | tf_op jit(solution)/shard_map/ppermute | solution.py:349
  45.1 33.3 %collective-permute-start.10 = (bf16[256,2048]{1,0:T(8,128)(2,1)}, bf16[256,2048]{1,0:T(8,128)(2,1)S(1)}, u32[]{:S(2)}, u32[]{:S(2)}) collective-permute-start(bf16[256,2048]{1,0:T(8,128)(2,1)} %get-tuple-element.74), channel_id=1, source_target_pairs={{0,1},{1,0},{2,3},{3,2},{4,5},{5,4},{6,7},{7,6},{8,9},{9,8},{10,11... | collective-permute-start | bytes 3145736 | tf_op jit(solution)/shard_map/ppermute | solution.py:349
  46.2 3.4 %collective-permute-start.4 = (bf16[256,256]{1,0:T(8,128)(2,1)S(1)}, bf16[256,256]{1,0:T(8,128)(2,1)S(1)}, u32[]{:S(2)}, u32[]{:S(2)}) collective-permute-start(bf16[256,256]{1,0:T(8,128)(2,1)S(1)} %copy-done.11), channel_id=1, source_target_pairs={{2,0},{3,1},{4,2},{5,3},{6,4},{7,5},{8,6},{9,7},{10,8},{11,9},{12,... | collective-permute-start | bytes 393224 | tf_op jit(solution)/shard_map/ppermute | solution.py:349
  49.7 14.1 %copy-start.6 = (bf16[256,256]{1,0:T(8,128)(2,1)}, bf16[256,256]{1,0:T(8,128)(2,1)S(1)}, u32[]{:S(2)}) copy-start(bf16[256,256]{1,0:T(8,128)(2,1)S(1)} %collective-permute-done.4.refs_11_.refs_7_) | copy-start | bytes 393220
  78.3 3.7 %copy-start.1 = (bf16[256,2048]{1,0:T(8,128)(2,1)}, bf16[256,2048]{1,0:T(8,128)(2,1)S(1)}, u32[]{:S(2)}) copy-start(bf16[256,2048]{1,0:T(8,128)(2,1)S(1)} %collective-permute-done.10.refs_0_.refs_1_.refs_2_) | copy-start | bytes 3145732
  78.3 6.2 %collective-permute-start.11 = (bf16[2,4,384,128]{3,2,1,0:T(8,128)(2,1)}, bf16[2,4,384,128]{3,2,1,0:T(8,128)(2,1)}, u32[]{:S(2)}, u32[]{:S(2)}) collective-permute-start(bf16[2,4,384,128]{3,2,1,0:T(8,128)(2,1)} %get-tuple-element.75), channel_id=1, source_target_pairs={{0,2},{1,3},{2,0},{3,1},{4,6},{5,7},{6,4},{7,5},{8,10},{9,11},{10,... | collective-permute-start | bytes 2359304 | tf_op jit(solution)/shard_map/ppermute | solution.py:349
  82.1 10.9 %collective-permute-start.5 = (bf16[4,1024,128]{2,1,0:T(8,128)(2,1)}, bf16[4,1024,128]{2,1,0:T(8,128)(2,1)}, u32[]{:S(2)}, u32[]{:S(2)}) collective-permute-start(bf16[4,1024,128]{2,1,0:T(8,128)(2,1)} %get-tuple-element.60), channel_id=1, source_target_pairs={{0,2},{1,3},{2,0},{3,1},{4,6},{5,7},{6,4},{7,5},{8,10},{9,11},{10,... | collective-permute-start | bytes 3145736 | tf_op jit(solution)/shard_map/ppermute | solution.py:349
  83.0 43.5 %collective-permute-start.13 = (bf16[384,2048]{1,0:T(8,128)(2,1)}, bf16[384,2048]{1,0:T(8,128)(2,1)S(1)}, u32[]{:S(2)}, u32[]{:S(2)}) collective-permute-start(bf16[384,2048]{1,0:T(8,128)(2,1)} %get-tuple-element.81), channel_id=1, source_target_pairs={{0,1},{1,0},{2,3},{3,2},{4,5},{5,4},{6,7},{7,6},{8,9},{9,8},{10,11... | collective-permute-start | bytes 4718600 | tf_op jit(solution)/shard_map/ppermute | solution.py:349
  87.7 25.9 %all-to-all-start = ((bf16[8,384,128]{2,1,0:T(8,128)(2,1)}), bf16[8,384,128]{2,1,0:T(8,128)(2,1)}, u32[]{:S(2)}, u32[]{:S(2)}) async-start(bf16[8,384,128]{2,1,0:T(8,128)(2,1)} %bitcast.33), calls=%async_computation | async-start | bytes 1572864 | tf_op jit(solution)/shard_map/all_to_all | solution.py:427
  105.7 2.3 %collective-permute-start.12 = (bf16[2,4,256,128]{3,2,1,0:T(8,128)(2,1)}, bf16[2,4,256,128]{3,2,1,0:T(8,128)(2,1)}, u32[]{:S(2)}, u32[]{:S(2)}) collective-permute-start(bf16[2,4,256,128]{3,2,1,0:T(8,128)(2,1)} %get-tuple-element.79), channel_id=1, source_target_pairs={{0,2},{1,3},{2,0},{3,1},{4,6},{5,7},{6,4},{7,5},{8,10},{9,11},{10,... | collective-permute-start | bytes 1572872 | tf_op jit(solution)/shard_map/ppermute | solution.py:349
  105.7 18.5 %collective-permute-start.6 = (bf16[2,1024,128]{2,1,0:T(8,128)(2,1)}, bf16[2,1024,128]{2,1,0:T(8,128)(2,1)}, u32[]{:S(2)}, u32[]{:S(2)}) collective-permute-start(bf16[2,1024,128]{2,1,0:T(8,128)(2,1)} %get-tuple-element.62), channel_id=1, source_target_pairs={{0,4},{1,5},{2,6},{3,7},{4,0},{5,1},{6,2},{7,3},{8,12},{9,13},{10,... | collective-permute-start | bytes 1572872 | tf_op jit(solution)/shard_map/ppermute | solution.py:349
  113.6 34.4 %all-to-all-start.1 = ((bf16[8,256,128]{2,1,0:T(8,128)(2,1)}), bf16[8,256,128]{2,1,0:T(8,128)(2,1)}, u32[]{:S(2)}, u32[]{:S(2)}) async-start(bf16[8,256,128]{2,1,0:T(8,128)(2,1)} %bitcast.35), calls=%async_computation.1 | async-start | bytes 1048576 | tf_op jit(solution)/shard_map/all_to_all | solution.py:427
  126.5 1.2 copy-start
  141.3 12.2 %copy-start.5 = (f32[384,128]{1,0:T(8,128)S(1)}, f32[384,128]{1,0:T(8,128)}, u32[]{:S(2)}) copy-start(f32[384,128]{1,0:T(8,128)} %gather_up_sums.3) | copy-start | bytes 589828
  141.3 2.5 %collective-permute-start.14 = (bf16[2,4,384,128]{3,2,1,0:T(8,128)(2,1)}, bf16[2,4,384,128]{3,2,1,0:T(8,128)(2,1)S(1)}, u32[]{:S(2)}, u32[]{:S(2)}) collective-permute-start(bf16[2,4,384,128]{3,2,1,0:T(8,128)(2,1)} %get-tuple-element.86), channel_id=1, source_target_pairs={{0,2},{1,3},{2,0},{3,1},{4,6},{5,7},{6,4},{7,5},{8,10},{9,11},{10,... | collective-permute-start | bytes 2359304 | tf_op jit(solution)/shard_map/ppermute | solution.py:349
  143.8 0.9 copy-start.7
  144.7 35.3 %copy-start.4 = (f32[1,1024,128]{2,1,0:T(8,128)S(1)}, f32[1,1024,128]{2,1,0:T(8,128)}, u32[]{:S(2)}) copy-start(f32[1,1024,128]{2,1,0:T(8,128)} %get-tuple-element.63) | copy-start | bytes 1572868
  148.0 26.1 %all-to-all-start.2 = ((bf16[8,384,128]{2,1,0:T(8,128)(2,1)}), bf16[8,384,128]{2,1,0:T(8,128)(2,1)S(1)}, u32[]{:S(2)}, u32[]{:S(2)}) async-start(bf16[8,384,128]{2,1,0:T(8,128)(2,1)} %bitcast.34), calls=%async_computation.2 | async-start | bytes 1572864 | tf_op jit(solution)/shard_map/all_to_all | solution.py:427
  157.7 19.3 %collective-permute-start.15 = (f32[8,80,128]{1,2,0:T(8,128)}, f32[8,80,128]{1,2,0:T(8,128)}, u32[]{:S(2)}, u32[]{:S(2)}) collective-permute-start(f32[8,80,128]{1,2,0:T(8,128)} %pad_maximum_fusion), channel_id=1, source_target_pairs={{0,1},{2,3},{4,5},{6,7},{8,9},{10,11},{12,13},{14,15},{17,16},{19,... | collective-permute-start | bytes 983048 | tf_op jit(solution)/shard_map/ppermute | solution.py:349
  161.5 18.5 %collective-permute-start.7 = (bf16[1,1024,128]{2,1,0:T(8,128)(2,1)}, bf16[1,1024,128]{2,1,0:T(8,128)(2,1)S(1)}, u32[]{:S(2)}, u32[]{:S(2)}) collective-permute-start(bf16[1,1024,128]{2,1,0:T(8,128)(2,1)} %get-tuple-element.64), channel_id=1, source_target_pairs={{0,8},{1,9},{2,10},{3,11},{4,12},{5,13},{6,14},{7,15},{8,0},{9,1},... | collective-permute-start | bytes 786440 | tf_op jit(solution)/shard_map/ppermute | solution.py:349
  174.1 0.9 copy-start.3
  176.9 6.6 %collective-permute-start.16 = (f32[8,48,128]{2,1,0:T(8,128)}, f32[8,48,128]{2,1,0:T(8,128)S(1)}, u32[]{:S(2)}, u32[]{:S(2)}) collective-permute-start(f32[8,48,128]{2,1,0:T(8,128)} %bitcast.40), channel_id=1, source_target_pairs={{0,1},{2,3},{4,5},{6,7},{8,9},{10,11},{12,13},{14,15},{17,16},{19,... | collective-permute-start | bytes 589832 | tf_op jit(solution)/shard_map/ppermute | solution.py:349
  180.1 14.2 %collective-permute-start.8 = (bf16[1024,128]{1,0:T(8,128)(2,1)S(1)}, bf16[1024,128]{1,0:T(8,128)(2,1)S(1)}, u32[]{:S(2)}, u32[]{:S(2)}) collective-permute-start(bf16[1024,128]{1,0:T(8,128)(2,1)S(1)} %bitcast_convert_fusion), channel_id=1, source_target_pairs={{1,17},{3,19},{5,21},{7,23},{9,25},{11,27},{13,29},{15,31},{16,0},... | collective-permute-start | bytes 786440 | tf_op jit(solution)/shard_map/ppermute | solution.py:349
